TPU v7x, 32 devices: a whole 2x2x4 slice. The times are simulated.
32 devices in a mesh: ctx: 4 (over y, x), fsdp: 8 (over z, core).
Axes of the slice: x: 2, y: 2, z: 4, core: 2. Of those that a mesh axis runs over, the one named last changes fastest.
Arguments:
- hidden_in: bfloat16 [8, 1024, 1536], P('fsdp', 'ctx'), may hold values from -6 to 6
- span_order: int32 [8], replicated, may hold values from 0 to 7, as said below
- routes: int32 [8, 1024, 8], P('fsdp', 'ctx'), may hold values from 0 to 15, all different within a row; in each aligned block of 256 rows (0 to 255, 256 to 511, ..., all dimensions but the last counted through in order) at most 160 rows name the same one
- attn_gain: bfloat16 [1536], P('fsdp'), may hold values from 0.5 to 1.5
- query_weight: bfloat16 [1536, 1536], P('fsdp'), may hold values from -150 to 150
- key_weight: bfloat16 [1536, 512], P('fsdp'), may hold values from -1 to 1
- value_weight: bfloat16 [1536, 512], P('fsdp'), may hold values from -0.15625 to 0.15625
- out_weight: bfloat16 [1536, 1536], P('fsdp'), may hold values from -6 to 6
- ffn_gain: bfloat16 [1536], P('fsdp'), may hold values from 0.5 to 1.5
- router_weight: bfloat16 [1536, 16], P('fsdp'), may hold values from -4 to 4
- gate_weight: bfloat16 [16, 1536, 512], P('fsdp'), may hold values from -0.15625 to 0.15625
- up_weight: bfloat16 [16, 1536, 512], P('fsdp'), may hold values from -0.15625 to 0.15625
- down_weight: bfloat16 [16, 1536, 512], P('fsdp'), may hold values from -3 to 3
- cotangent: bfloat16 [8, 1024, 1536], P('fsdp', 'ctx'), may hold values from -6 to 6
Outputs:
- hidden_out: bfloat16 [8, 1024, 1536], P('fsdp', 'ctx')
- grad_in: float32 [8, 1024, 1536], P('fsdp', 'ctx')
- grad_attn_gain: float32 [1536], P(('ctx', 'fsdp'))
- grad_query: float32 [1536, 1536], P(('ctx', 'fsdp'))
- grad_key: float32 [1536, 512], P(('ctx', 'fsdp'))
- grad_value: float32 [1536, 512], P(('ctx', 'fsdp'))
- grad_out: float32 [1536, 1536], P(('ctx', 'fsdp'))
- grad_ffn_gain: float32 [1536], P(('ctx', 'fsdp'))
- grad_router: float32 [1536, 16], P(('ctx', 'fsdp'))
- grad_gate: float32 [16, 1536, 512], P('fsdp', 'ctx')
- grad_up: float32 [16, 1536, 512], P('fsdp', 'ctx')
- grad_down: float32 [16, 1536, 512], P('fsdp', 'ctx')
Inputs may be any that keep to these rules, and one draw needn't show every extreme that they name: `span_order`: stored spans 2c and 2c + 1 hold spans p and 7 - p, in that order, for some p below 4; every span appears once. `routes`: the 8 experts of a token differ. Among the rows of one device no expert is named more than 160 times, and in every draw some expert is named exactly 160 times on some device.
All inputs are finite; a program needn't handle non-finite values.
Results may differ from a plain program's by a relative error of at most 0.018.
Values may be sent and summed in bfloat16 or wider, within the bound.
No kernel may reach another device: no remote copies, remote signals or barrier semaphores. Data moves between devices by JAX's collectives and lax.ppermute only.
A program may use at most 320 MiB of HBM per device.

v0:
```python
import math

import jax
import jax.numpy as jnp
from jax import lax
from jax.sharding import PartitionSpec as P

HEAD = 64


NORM_EPS = 1e-06
ATTN_SCALE = 0.015625
RESID_SCALE = 0.22
ROPE_THETA = 10000.0
MASKED_SCORE = -1e30
HIGHEST = lax.Precision.HIGHEST
CONTRACT_LAST = (((1,), (1,)), ((), ()))
CONTRACT_FIRST = (((0,), (0,)), ((), ()))


def rope_tables(positions, head_size):
    half_size = head_size // 2
    frequencies = ROPE_THETA ** (-2.0 * jnp.arange(half_size, dtype=jnp.float32) / head_size)
    angles = positions.astype(jnp.float32)[:, None] * frequencies[None, :]
    return (jnp.cos(angles)[:, None, :], jnp.sin(angles)[:, None, :])


def rotate(rope_field, cosine_table, sine_table):
    half_size = rope_field.shape[-1] // 2
    front_half = rope_field[..., :half_size]
    back_half = rope_field[..., half_size:]
    return jnp.concatenate(
        [
            front_half * cosine_table - back_half * sine_table,
            back_half * cosine_table + front_half * sine_table,
        ],
        axis=-1,
    )


def unrotate(grad_field, cosine_table, sine_table):
    half_size = grad_field.shape[-1] // 2
    front_half = grad_field[..., :half_size]
    back_half = grad_field[..., half_size:]
    return jnp.concatenate(
        [
            front_half * cosine_table + back_half * sine_table,
            back_half * cosine_table - front_half * sine_table,
        ],
        axis=-1,
    )


def norm_back(grad_normed, normed, scale):
    return scale * (grad_normed - normed * jnp.mean(grad_normed * normed, axis=-1, keepdims=True))


def positions_of(row_ids, span_order, half_block):
    span_ids = row_ids // half_block
    span_table = span_ids[:, None] == jnp.arange(span_order.shape[0], dtype=jnp.int32)[None, :]
    return (
        jnp.sum(jnp.where(span_table, span_order[None, :], 0), axis=1) * half_block
        + row_ids % half_block
    )


def slot_maps(route_rows, expert_count, capacity):
    flat_routes = route_rows.reshape(-1)
    expert_hits = (
        flat_routes[:, None] == jnp.arange(expert_count, dtype=jnp.int32)[None, :]
    ).astype(jnp.int32)
    slot_ranks = jnp.sum((jnp.cumsum(expert_hits, axis=0) - 1) * expert_hits, axis=1)
    slot_of_pair = flat_routes * capacity + slot_ranks
    pair_token = jnp.arange(flat_routes.shape[0], dtype=jnp.int32) // route_rows.shape[1]
    slot_token = jnp.zeros((expert_count * capacity,), jnp.int32).at[slot_of_pair].set(pair_token)
    slot_used = jnp.zeros((expert_count * capacity,), jnp.int32).at[slot_of_pair].set(1)
    return (slot_of_pair, slot_token, slot_used)


def expert_forward(dispatched, w_gate, w_up, w_down):
    gate_act = jnp.einsum("ecd,edf->ecf", dispatched, w_gate, preferred_element_type=jnp.float32)
    up_act = jnp.einsum("ecd,edf->ecf", dispatched, w_up, preferred_element_type=jnp.float32)
    hidden = (jax.nn.silu(gate_act) * up_act).astype(jnp.bfloat16)
    expert_out = jnp.einsum(
        "ecf,edf->ecd", hidden, w_down, preferred_element_type=jnp.float32
    ).astype(jnp.bfloat16)
    return (gate_act, up_act, expert_out)


def expert_backward(grad_slots, gate_act, up_act, w_gate, w_up, w_down):
    grad_hidden = jnp.einsum("ecd,edf->ecf", grad_slots, w_down, preferred_element_type=jnp.float32)
    sigmoid_gate = jax.nn.sigmoid(gate_act)
    silu_act = gate_act * sigmoid_gate
    hidden = (silu_act * up_act).astype(jnp.bfloat16)
    grad_gate_act = (
        grad_hidden * up_act * sigmoid_gate * (1.0 + gate_act * (1.0 - sigmoid_gate))
    ).astype(jnp.bfloat16)
    grad_up_act = (grad_hidden * silu_act).astype(jnp.bfloat16)
    grad_slot_in = jnp.einsum(
        "ecf,edf->ecd", grad_gate_act, w_gate, preferred_element_type=jnp.float32
    )
    grad_slot_in = (
        grad_slot_in
        + jnp.einsum("ecf,edf->ecd", grad_up_act, w_up, preferred_element_type=jnp.float32)
    ).astype(jnp.bfloat16)
    return (grad_slot_in, grad_gate_act, grad_up_act, hidden)


def expert_terms(dispatched, grad_slots, grad_gate_act, grad_up_act, hidden):
    return jnp.concatenate(
        [
            jnp.einsum(
                "ecd,ecf->edf", dispatched, grad_gate_act, preferred_element_type=jnp.float32
            ),
            jnp.einsum("ecd,ecf->edf", dispatched, grad_up_act, preferred_element_type=jnp.float32),
            jnp.einsum("ecd,ecf->edf", grad_slots, hidden, preferred_element_type=jnp.float32),
        ],
        axis=2,
    )


def blocks_of(key_total):
    block_size = math.gcd(key_total, 512)
    return (block_size, key_total // block_size)


def body(
    hidden_in,
    span_order,
    routes,
    attn_gain,
    query_weight,
    key_weight,
    value_weight,
    out_weight,
    ffn_gain,
    router_weight,
    gate_weight,
    up_weight,
    down_weight,
    cotangent,
):
    local_rows = hidden_in.shape[1]
    model_width = hidden_in.shape[2]
    head_count = query_weight.shape[1] // HEAD
    kv_count = key_weight.shape[1] // HEAD
    group_size = head_count // kv_count
    kv_width = key_weight.shape[1]
    expert_count = router_weight.shape[1]
    top_count = routes.shape[2]
    hidden_units = gate_weight.shape[2]
    capacity = local_rows * top_count * 5 // (4 * expert_count)
    half_block = local_rows // 2
    ctx_count = lax.axis_size("ctx")
    inputs = hidden_in[0].astype(jnp.float32)
    gain_one, w_query, w_key, w_value, w_out, gain_two, w_router = (
        lax.all_gather(attn_gain, "fsdp", axis=0, tiled=True),
        lax.all_gather(query_weight, "fsdp", axis=0, tiled=True),
        lax.all_gather(key_weight, "fsdp", axis=0, tiled=True),
        lax.all_gather(value_weight, "fsdp", axis=0, tiled=True),
        lax.all_gather(out_weight, "fsdp", axis=0, tiled=True),
        lax.all_gather(ffn_gain, "fsdp", axis=0, tiled=True),
        lax.all_gather(router_weight, "fsdp", axis=0, tiled=True),
    )
    gain_one = gain_one.astype(jnp.float32)
    gain_two = gain_two.astype(jnp.float32)
    own_rows = lax.axis_index("ctx") * local_rows + jnp.arange(local_rows, dtype=jnp.int32)
    own_pos = positions_of(own_rows, span_order, half_block)
    cosine_table, sine_table = rope_tables(own_pos, HEAD)
    scale_one = lax.rsqrt(jnp.mean(inputs * inputs, axis=-1, keepdims=True) + NORM_EPS)
    normed_one = inputs * scale_one
    attn_in = (normed_one * gain_one).astype(jnp.bfloat16)
    query_lin = jnp.dot(attn_in, w_query, preferred_element_type=jnp.float32).reshape(
        local_rows, head_count, HEAD
    )
    key_lin = jnp.dot(attn_in, w_key, preferred_element_type=jnp.float32).reshape(
        local_rows, kv_count, HEAD
    )
    value_rows = jnp.dot(attn_in, w_value, preferred_element_type=jnp.float32).astype(jnp.bfloat16)
    query_rot = (
        rotate(query_lin, cosine_table, sine_table)
        .astype(jnp.bfloat16)
        .reshape(local_rows, kv_count, group_size, HEAD)
    )
    key_rot = (
        rotate(key_lin, cosine_table, sine_table).astype(jnp.bfloat16).reshape(local_rows, kv_width)
    )

    def visible(block_start, key_count):
        key_pos = positions_of(
            block_start + jnp.arange(key_count, dtype=jnp.int32), span_order, half_block
        )
        return own_pos[:, None] >= key_pos[None, :]

    def forward_block(running, key_block, value_block, block_start):
        key_count = key_block.shape[0]
        allowed = visible(block_start, key_count)
        row_max, row_total, weighted, weighted_exact = running
        values_split = value_block.reshape(key_count, kv_count, HEAD)
        raw_scores = jnp.einsum(
            "tkgd,skd->kgts",
            query_rot,
            key_block.reshape(key_count, kv_count, HEAD),
            preferred_element_type=jnp.float32,
        )
        scores = jnp.where(allowed, raw_scores * ATTN_SCALE, MASKED_SCORE)
        new_max = jnp.maximum(row_max, jnp.max(scores, axis=-1))
        weights = jnp.where(allowed, jnp.exp(scores - new_max[..., None]), 0.0)
        shrink = jnp.exp(row_max - new_max)
        row_total = row_total * shrink + jnp.sum(weights, axis=-1)
        weighted = weighted * shrink[..., None] + jnp.einsum(
            "kgts,skd->kgtd",
            weights.astype(jnp.bfloat16),
            values_split,
            preferred_element_type=jnp.float32,
        )
        weighted_exact = weighted_exact * shrink[..., None] + jnp.einsum(
            "kgts,skd->kgtd", weights, values_split.astype(jnp.float32), precision=HIGHEST
        )
        return (new_max, row_total, weighted, weighted_exact)

    start_state = (
        jnp.full((kv_count, group_size, local_rows), MASKED_SCORE, jnp.float32),
        jnp.zeros((kv_count, group_size, local_rows), jnp.float32),
        jnp.zeros((kv_count, group_size, local_rows, HEAD), jnp.float32),
        jnp.zeros((kv_count, group_size, local_rows, HEAD), jnp.float32),
    )
    key_piece = lax.all_gather(key_rot, "ctx", axis=0, tiled=True)
    value_piece = lax.all_gather(value_rows, "ctx", axis=0, tiled=True)
    block_size, block_count = blocks_of(key_piece.shape[0])

    def one_block(block_index, current):
        offset = block_index * block_size
        return forward_block(
            current,
            lax.dynamic_slice_in_dim(key_piece, offset, block_size, 0),
            lax.dynamic_slice_in_dim(value_piece, offset, block_size, 0),
            offset,
        )

    row_max, row_total, weighted, weighted_exact = lax.fori_loop(
        0, block_count, one_block, start_state
    )
    attn_full = weighted / row_total[..., None]
    attn_exact = weighted_exact / row_total[..., None]
    log_total = row_max + jnp.log(row_total)
    attn_mix = (
        attn_full.transpose(2, 0, 1, 3).reshape(local_rows, head_count * HEAD).astype(jnp.bfloat16)
    )
    branch = lax.dot_general(attn_mix, w_out, CONTRACT_LAST, preferred_element_type=jnp.float32)
    after_attn = inputs + RESID_SCALE * branch
    scale_two = lax.rsqrt(jnp.mean(after_attn * after_attn, axis=-1, keepdims=True) + NORM_EPS)
    normed_two = after_attn * scale_two
    ffn_in = (normed_two * gain_two).astype(jnp.bfloat16)
    router_probs = jax.nn.softmax(
        jnp.dot(ffn_in, w_router, preferred_element_type=jnp.float32), axis=-1
    )
    route_rows = routes[0]
    route_hits = route_rows[:, :, None] == jnp.arange(expert_count, dtype=jnp.int32)[None, None, :]
    combine = jnp.sum(jnp.where(route_hits, router_probs[:, None, :], 0.0), axis=-1)
    slot_of_pair, slot_token, slot_used = slot_maps(route_rows, expert_count, capacity)
    dispatched = (ffn_in[slot_token] * slot_used[:, None].astype(jnp.bfloat16)).reshape(
        expert_count, capacity, model_width
    )
    received = lax.all_to_all(dispatched, "fsdp", split_axis=0, concat_axis=1, tiled=True)
    gate_act, up_act, local_out = expert_forward(received, gate_weight, up_weight, down_weight)
    expert_out = lax.all_to_all(local_out, "fsdp", split_axis=1, concat_axis=0, tiled=True)
    picked = expert_out.reshape(expert_count * capacity, model_width)[slot_of_pair].reshape(
        local_rows, top_count, model_width
    )
    mixture = jnp.sum(combine[:, :, None] * picked.astype(jnp.float32), axis=1)
    hidden_out = (after_attn + RESID_SCALE * mixture).astype(jnp.bfloat16)[None]
    grad_rows_out = cotangent[0].astype(jnp.float32)
    grad_mixture = RESID_SCALE * grad_rows_out
    grad_picked = (combine[:, :, None] * grad_mixture[:, None, :]).astype(jnp.bfloat16)
    grad_combine = jnp.sum(grad_mixture[:, None, :] * picked.astype(jnp.float32), axis=-1)
    grad_slots = (
        jnp.zeros((expert_count * capacity, model_width), jnp.bfloat16)
        .at[slot_of_pair]
        .set(grad_picked.reshape(-1, model_width))
        .reshape(expert_count, capacity, model_width)
    )
    grad_received = lax.all_to_all(grad_slots, "fsdp", split_axis=0, concat_axis=1, tiled=True)
    local_grad_in, grad_gate_act, grad_up_act, hidden = expert_backward(
        grad_received, gate_act, up_act, gate_weight, up_weight, down_weight
    )
    partial_terms = expert_terms(received, grad_received, grad_gate_act, grad_up_act, hidden)
    grad_slot_in = lax.all_to_all(local_grad_in, "fsdp", split_axis=1, concat_axis=0, tiled=True)
    expert_sums = lax.psum_scatter(
        partial_terms.astype(jnp.bfloat16), "ctx", scatter_dimension=1, tiled=True
    ).astype(jnp.float32)
    grad_pairs = grad_slot_in.reshape(expert_count * capacity, model_width)[slot_of_pair].reshape(
        local_rows, top_count, model_width
    )
    router_grad_probs = jnp.sum(jnp.where(route_hits, grad_combine[:, :, None], 0.0), axis=1)
    grad_logits = router_probs * (
        router_grad_probs - jnp.sum(router_probs * router_grad_probs, axis=-1, keepdims=True)
    )
    grad_ffn_in = jnp.sum(grad_pairs.astype(jnp.float32), axis=1) + lax.dot_general(
        grad_logits, w_router.astype(jnp.float32), CONTRACT_LAST, precision=HIGHEST
    )
    grad_gain_two = jnp.sum(grad_ffn_in * normed_two, axis=0)
    grad_after = grad_rows_out + norm_back(grad_ffn_in * gain_two, normed_two, scale_two)
    grad_branch = (RESID_SCALE * grad_after).astype(jnp.bfloat16)
    grad_mix = jnp.dot(grad_branch, w_out, preferred_element_type=jnp.float32).astype(jnp.bfloat16)
    grad_heads = grad_mix.reshape(local_rows, kv_count, group_size, HEAD).transpose(1, 2, 0, 3)
    row_delta = jnp.sum(grad_heads.astype(jnp.float32) * attn_exact, axis=-1)

    def backward_block(running, key_block, value_block, block_start):
        key_count = key_block.shape[0]
        allowed = visible(block_start, key_count)
        grad_query_acc, grad_key_all, grad_value_all = running
        keys_split = key_block.reshape(key_count, kv_count, HEAD)
        values_split = value_block.reshape(key_count, kv_count, HEAD)
        raw_scores = jnp.einsum(
            "tkgd,skd->kgts", query_rot, keys_split, preferred_element_type=jnp.float32
        )
        scores = jnp.where(allowed, raw_scores * ATTN_SCALE, MASKED_SCORE)
        weights = jnp.where(allowed, jnp.exp(scores - log_total[..., None]), 0.0)
        grad_weights = jnp.einsum(
            "kgtd,skd->kgts", grad_heads, values_split, preferred_element_type=jnp.float32
        )
        grad_raw = (weights * (grad_weights - row_delta[..., None]) * ATTN_SCALE).astype(
            jnp.bfloat16
        )
        grad_query_acc = grad_query_acc + jnp.einsum(
            "kgts,skd->kgtd", grad_raw, keys_split, preferred_element_type=jnp.float32
        )
        key_part = jnp.einsum(
            "kgts,tkgd->skd", grad_raw, query_rot, preferred_element_type=jnp.float32
        ).reshape(key_count, kv_width)
        value_part = jnp.einsum(
            "kgts,kgtd->skd",
            weights.astype(jnp.bfloat16),
            grad_heads,
            preferred_element_type=jnp.float32,
        ).reshape(key_count, kv_width)
        grad_key_all = lax.dynamic_update_slice_in_dim(
            grad_key_all,
            lax.dynamic_slice_in_dim(grad_key_all, block_start, key_count, 0) + key_part,
            block_start,
            0,
        )
        grad_value_all = lax.dynamic_update_slice_in_dim(
            grad_value_all,
            lax.dynamic_slice_in_dim(grad_value_all, block_start, key_count, 0) + value_part,
            block_start,
            0,
        )
        return (grad_query_acc, grad_key_all, grad_value_all)

    start_back = (
        jnp.zeros((kv_count, group_size, local_rows, HEAD), jnp.float32),
        jnp.zeros((ctx_count * local_rows, kv_width), jnp.float32),
        jnp.zeros((ctx_count * local_rows, kv_width), jnp.float32),
    )
    fold_key_piece = lax.all_gather(key_rot, "ctx", axis=0, tiled=True)
    fold_value_piece = lax.all_gather(value_rows, "ctx", axis=0, tiled=True)
    fold_block_size, block_count = blocks_of(fold_key_piece.shape[0])

    def one_block(block_index, current):
        offset = block_index * fold_block_size
        return backward_block(
            current,
            lax.dynamic_slice_in_dim(fold_key_piece, offset, fold_block_size, 0),
            lax.dynamic_slice_in_dim(fold_value_piece, offset, fold_block_size, 0),
            offset,
        )

    grad_query_acc, grad_key_all, grad_value_all = lax.fori_loop(
        0, block_count, one_block, start_back
    )
    grad_key_sum, grad_value_sum = (
        lax.psum_scatter(
            grad_key_all.astype(jnp.bfloat16), "ctx", scatter_dimension=0, tiled=True
        ).astype(jnp.float32),
        lax.psum_scatter(
            grad_value_all.astype(jnp.bfloat16), "ctx", scatter_dimension=0, tiled=True
        ).astype(jnp.float32),
    )
    grad_query_lin = (
        unrotate(
            grad_query_acc.transpose(2, 0, 1, 3).reshape(local_rows, head_count, HEAD),
            cosine_table,
            sine_table,
        )
        .reshape(local_rows, head_count * HEAD)
        .astype(jnp.bfloat16)
    )
    grad_key_lin = (
        unrotate(grad_key_sum.reshape(local_rows, kv_count, HEAD), cosine_table, sine_table)
        .reshape(local_rows, kv_width)
        .astype(jnp.bfloat16)
    )
    grad_value_lin = grad_value_sum.astype(jnp.bfloat16)
    grad_attn_in = lax.dot_general(
        grad_query_lin, w_query, CONTRACT_LAST, preferred_element_type=jnp.float32
    )
    grad_attn_in = grad_attn_in + lax.dot_general(
        grad_key_lin, w_key, CONTRACT_LAST, preferred_element_type=jnp.float32
    )
    grad_attn_in = grad_attn_in + lax.dot_general(
        grad_value_lin, w_value, CONTRACT_LAST, preferred_element_type=jnp.float32
    )
    grad_gain_one = jnp.sum(grad_attn_in * normed_one, axis=0)
    grad_in = (grad_after + norm_back(grad_attn_in * gain_one, normed_one, scale_one))[None]
    attn_sums = lax.psum_scatter(
        jnp.concatenate(
            [
                lax.dot_general(
                    attn_in, grad_query_lin, CONTRACT_FIRST, preferred_element_type=jnp.float32
                ),
                lax.dot_general(
                    attn_in, grad_key_lin, CONTRACT_FIRST, preferred_element_type=jnp.float32
                ),
                lax.dot_general(
                    attn_in, grad_value_lin, CONTRACT_FIRST, preferred_element_type=jnp.float32
                ),
                lax.dot_general(
                    grad_branch, attn_mix, CONTRACT_FIRST, preferred_element_type=jnp.float32
                ),
                lax.dot_general(
                    ffn_in.astype(jnp.float32), grad_logits, CONTRACT_FIRST, precision=HIGHEST
                ),
                grad_gain_one[:, None],
                grad_gain_two[:, None],
            ],
            axis=1,
        ),
        ("ctx", "fsdp"),
        scatter_dimension=0,
        tiled=True,
    )
    query_cols = head_count * HEAD
    edge_key = query_cols + kv_width
    edge_value = edge_key + kv_width
    edge_out = edge_value + query_cols
    edge_router = edge_out + expert_count
    grad_query = attn_sums[:, :query_cols]
    grad_key = attn_sums[:, query_cols:edge_key]
    grad_value = attn_sums[:, edge_key:edge_value]
    grad_out = attn_sums[:, edge_value:edge_out]
    grad_router = attn_sums[:, edge_out:edge_router]
    grad_attn_gain = attn_sums[:, edge_router]
    grad_ffn_gain = attn_sums[:, edge_router + 1]
    grad_gate = expert_sums[:, :, :hidden_units]
    grad_up = expert_sums[:, :, hidden_units : 2 * hidden_units]
    grad_down = expert_sums[:, :, 2 * hidden_units :]
    return (
        hidden_out,
        grad_in,
        grad_attn_gain,
        grad_query,
        grad_key,
        grad_value,
        grad_out,
        grad_ffn_gain,
        grad_router,
        grad_gate,
        grad_up,
        grad_down,
    )


def solution(mesh):
    return jax.shard_map(
        body,
        mesh=mesh,
        in_specs=(
            P("fsdp", "ctx", None),
            P(),
            P("fsdp", "ctx", None),
            P("fsdp"),
            P("fsdp", None),
            P("fsdp", None),
            P("fsdp", None),
            P("fsdp", None),
            P("fsdp"),
            P("fsdp", None),
            P("fsdp", None, None),
            P("fsdp", None, None),
            P("fsdp", None, None),
            P("fsdp", "ctx", None),
        ),
        out_specs=(
            P("fsdp", "ctx", None),
            P("fsdp", "ctx", None),
            P(("ctx", "fsdp")),
            P(("ctx", "fsdp"), None),
            P(("ctx", "fsdp"), None),
            P(("ctx", "fsdp"), None),
            P(("ctx", "fsdp"), None),
            P(("ctx", "fsdp")),
            P(("ctx", "fsdp"), None),
            P("fsdp", "ctx", None),
            P("fsdp", "ctx", None),
            P("fsdp", "ctx", None),
        ),
        check_vma=False,
    )
```

profile of v0, /device:TPU:0, one launch (start us, length us, event | category | flops | bytes accessed | tf_op | source)
XLA Modules:
  0.0 1620.0 jit_solution(3017760256691524946)
XLA Ops:
  12.4 18.7 %all-reduce.2 = (bf16[1536]{0:T(1024)(128)(2,1)S(1)}, bf16[1536]{0:T(1024)(128)(2,1)S(1)}) all-reduce(bf16[1536]{0:T(1024)(128)(2,1)S(1)} %dynamic-update-slice, bf16[1536]{0:T(1024)(128)(2,1)S(1)} %dynamic-update-slice.1), channel_id=1, replica_groups=mesh['ctx'=4,'fsdp'=8] {'fsdp'}, use_global_device_ids=true, to_apply=%add | all-reduce | flops 3072 | bytes 12288
  42.3 21.6 %all-gather.8.cloned.1.call-done = bf16[1536,512]{1,0:T(8,128)(2,1)} async-done(((bf16[192,512]{1,0:T(8,128)(2,1)}), bf16[1536,512]{1,0:T(8,128)(2,1)}) %all-gather.8.cloned.1.call-update) | async-done | bytes 1572880 | tf_op jit(solution)/shard_map/all_gather | solution.py:159
  72.4 14.0 all-gather
  102.5 43.3 %all-gather.12.cloned.1.call-done = bf16[1536,1536]{1,0:T(8,128)(2,1)} async-done(((bf16[192,1536]{1,0:T(8,128)(2,1)}), bf16[1536,1536]{1,0:T(8,128)(2,1)}) %all-gather.12.cloned.1.call-update) | async-done | bytes 4718608 | tf_op jit(solution)/shard_map/all_gather | solution.py:158
  158.0 15.4 all-gather.10.cloned.1.call-done
  173.4 71.7 %while.42 = (s32[]{:T(128)}, f32[8,3,256]{2,1,0:T(4,128)S(1)}, f32[8,3,256]{2,1,0:T(4,128)S(1)}, f32[8,3,256,64]{2,3,1,0:T(8,128)}, f32[8,3,256,64]{2,3,1,0:T(8,...) while((s32[]{:T(128)}, f32[8,3,256]{2,1,0:T(4,128)S(1)}, ...), condition=%wide.region_6.7_spmd.clone, body=%wide.region_2.6_spmd.clone.sunk | while | flops 3277251072 | bytes 89453936 | solution.py:241
  190.4 10.7 fusion.196
  226.0 10.6 fusion.196
  253.9 15.4 scatter_custom_fusion.2
  290.5 17.6 %gather_fusion = bf16[2560,1536]{1,0:T(8,128)(2,1)} fusion(bf16[256,1536]{1,0:T(8,128)(2,1)} %copy-done.2, s32[3072]{0:T(1024)S(1)} %pad_clamp_fusion), kind=kCustom, calls=%fused_computation | custom fusion | bytes 15738880 | tf_op jit(solution)/shard_map/gather | solution.py:262
  315.0 131.9 %all-to-all-done.2 = bf16[16,160,1536]{2,1,0:T(8,128)(2,1)} async-done(((bf16[16,160,1536]{2,1,0:T(8,128)(2,1)}), bf16[16,160,1536]{2,1,0:T(8,128)(2,1)}, u32[]{:S(2)}, u32[]{:S(2)}) %all-to-all-start.2) | async-done | bytes 7864352 | tf_op jit(solution)/shard_map/all_to_all | solution.py:283
  459.1 165.5 %all-to-all-done = bf16[16,160,1536]{2,1,0:T(8,128)(2,1)} async-done(((bf16[16,160,1536]{2,1,0:T(8,128)(2,1)}), bf16[16,160,1536]{2,1,0:T(8,128)(2,1)}, u32[]{:S(2)}, u32[]{:S(2)}) %all-to-all-start) | async-done | bytes 7864352 | tf_op jit(solution)/shard_map/all_to_all | solution.py:265
  631.8 9.4 fusion.105
  647.3 10.7 multiply_convert_fusion
  662.6 43.7 %copy.158 = bf16[2,1280,1536]{2,0,1:T(2,128)(2,1)} copy(bf16[2,1280,1536]{2,1,0:T(8,128)(2,1)S(1)} %convolution_convert_fusion) | data formatting | bytes 15728640 | tf_op jit(solution)/shard_map/convert_element_type | solution.py:86
  711.6 9.5 fusion.107
  721.2 14.6 add_convert_fusion
  735.8 15.6 copy.162
  751.4 132.9 %all-to-all-done.1 = bf16[2,1280,1536]{2,0,1:T(2,128)(2,1)} async-done(((bf16[2,1280,1536]{2,0,1:T(2,128)(2,1)}), bf16[2,1280,1536]{2,0,1:T(2,128)(2,1)}, u32[]{:S(2)}, u32[]{:S(2)}) %all-to-all-start.1) | async-done | bytes 7864352 | tf_op jit(solution)/shard_map/all_to_all | solution.py:267
  897.4 17.9 %gather_fusion.1 = bf16[2048,1536]{1,0:T(8,128)(2,1)} fusion(bf16[2560,1536]{1,0:T(8,128)(2,1)} %bitcast.300, s32[2048]{0:T(1024)S(1)} %broadcast_clamp_fusion), kind=kCustom, calls=%fused_computation.1 | custom fusion | bytes 12591104 | tf_op jit(solution)/shard_map/gather | solution.py:268
  915.3 9.5 fusion.37
  924.9 137.0 %all-to-all-done.3 = bf16[2,1280,1536]{2,0,1:T(2,128)(2,1)} async-done(((bf16[2,1280,1536]{2,0,1:T(2,128)(2,1)}), bf16[2,1280,1536]{2,0,1:T(2,128)(2,1)}, u32[]{:S(2)}, u32[]{:S(2)}) %all-to-all-start.3) | async-done | bytes 7864352 | tf_op jit(solution)/shard_map/all_to_all | solution.py:288
  1069.8 18.0 %gather_fusion.2 = bf16[2048,1536]{1,0:T(8,128)(2,1)} fusion(bf16[2560,1536]{1,0:T(8,128)(2,1)} %bitcast.299, s32[2048]{0:T(1024)S(1)} %broadcast_clamp_fusion), kind=kCustom, calls=%fused_computation.2 | custom fusion | bytes 12591104 | tf_op jit(solution)/shard_map/gather | solution.py:292
  1105.2 58.6 %while.43 = (s32[]{:T(128)}, f32[8,3,256,64]{2,3,1,0:T(8,128)}, f32[1024,512]{0,1:T(8,128)}, f32[1024,512]{0,1:T(8,128)}, s32[256]{0:T(256)S(1)}, /*index=5*/s32...) while((s32[]{:T(128)}, f32[8,3,256,64]{2,3,1,0:T(8,128)}, ...), condition=%wide.region_26.27_spmd.clone, body=%wide.region_24.26_spmd.clone.sunk | while | flops 2055629312 | bytes 106911056 | solution.py:370
  1166.6 10.0 convolution_convert_fusion.1
  1178.0 8.4 convolution_convert_fusion.2
  1186.4 10.1 convolution_convert_fusion.3
  1202.7 24.1 %copy.193 = bf16[2,1536,1536]{2,0,1:T(2,128)(2,1)} copy(bf16[2,1536,1536]{1,2,0:T(8,128)(2,1)} %pad_maximum_fusion) | data formatting | bytes 18874368
  1226.7 9.8 copy.203
  1267.7 61.3 %concatenate.32 = f32[1536,4114]{0,1:T(8,128)} concatenate(f32[1536,1536]{0,1:T(8,128)} %fusion.67, f32[1536,512]{0,1:T(8,128)} %fusion.69, f32[1536,512]{0,1:T(8,128)} %fusion.72, f32[1536,1536]{0,1:T(8,128)} %fusion.71, f32[1536,16]{0,1:T(8,128)S(1)} %fusion.87, f32[1536,1]{0,1:T(1,128)S(1)} %broadcast_in_dim.267, f32[1536,1]{0,1:T(1,128)S(1)} %broadcast_in_dim.268), dimensions={1} | concatenate | bytes 50552832 | tf_op jit(solution)/shard_map/concatenate | solution.py:408
  1328.9 25.9 %copy.191 = f32[1536,4114]{1,0:T(8,128)} copy(f32[1536,4114]{0,1:T(8,128)} %concatenate.32) | data formatting | bytes 50552832
  1382.4 223.3 %reduce-scatter.13.cloned.1.call-done = f32[48,4114]{1,0:T(8,128)} async-done(((f32[1536,4114]{1,0:T(8,128)}), f32[48,4114]{1,0:T(8,128)}) %reduce-scatter.13.cloned.1.call-update) | async-done | bytes 789904
  (345 shorter events, 346.5 us)
Async XLA Ops:
  7.2 640.1 %copy-start = (bf16[2,1536,512]{2,1,0:T(8,128)(2,1)S(1)}, bf16[2,1536,512]{2,1,0:T(8,128)(2,1)}, u32[]{:S(2)}) copy-start(bf16[2,1536,512]{2,1,0:T(8,128)(2,1)} %param.30) | copy-start | bytes 9437188
  7.2 34.2 %copy-start.47 = (s32[8]{0:T(128)S(1)}, s32[8]{0:T(128)}, u32[]{:S(2)}) copy-start(s32[8]{0:T(128)} %param.19) | copy-start | bytes 100
  7.2 30.5 %all-gather.14.cloned.1.call-start = ((), (), s32[]{:S(2)}) async-start(), calls=%async_computation.11 | async-start | bytes 1769472 | tf_op jit(solution)/shard_map/all_gather | solution.py:160
  7.9 55.9 %all-gather.8.cloned.1.call-start = ((), (), s32[]{:S(2)}) async-start(), calls=%async_computation.8 | async-start | bytes 1769472 | tf_op jit(solution)/shard_map/all_gather | solution.py:159
  8.7 91.5 %all-gather.16.cloned.1.call-start = ((), (), s32[]{:S(2)}) async-start(), calls=%async_computation.12 | async-start | bytes 1310720 | tf_op jit(solution)/shard_map/all_gather | solution.py:229
  31.1 121.3 %copy-start.34 = (f32[1536]{0:T(1024)}, f32[1536]{0:T(1024)S(1)}, u32[]{:S(2)}) copy-start(f32[1536]{0:T(1024)S(1)} %convert_element_type.203) | copy-start | bytes 18436
  32.5 33.9 %copy-start.50 = (f32[256]{0:T(256)}, f32[256]{0:T(256)S(1)}, u32[]{:S(2)}) copy-start(f32[256]{0:T(256)S(1)} %add_rsqrt_fusion.1) | copy-start | bytes 3076
  40.7 105.1 %all-gather.12.cloned.1.call-start = ((), (), s32[]{:S(2)}) async-start(), calls=%async_computation.10 | async-start | bytes 5308416 | tf_op jit(solution)/shard_map/all_gather | solution.py:158
  41.3 132.0 %all-gather.10.cloned.1.call-start = ((), (), s32[]{:S(2)}) async-start(), calls=%async_computation.9 | async-start | bytes 1310720 | tf_op jit(solution)/shard_map/all_gather | solution.py:228
  42.3 114.4 %copy-start.28 = (f32[256,32]{0,1:T(8,128)}, f32[256,32]{0,1:T(8,128)S(1)}, u32[]{:S(2)}) copy-start(f32[256,32]{0,1:T(8,128)S(1)} %get-tuple-element.884) | copy-start | bytes 98308
  42.3 114.4 %copy-start.30 = (f32[256,32]{0,1:T(8,128)}, f32[256,32]{0,1:T(8,128)S(1)}, u32[]{:S(2)}) copy-start(f32[256,32]{0,1:T(8,128)S(1)} %get-tuple-element.885) | copy-start | bytes 98308
  69.6 177.9 %all-gather.18.cloned.1.call-start = ((), (), s32[]{:S(2)}) async-start(), calls=%async_computation.13 | async-start | bytes 5308416 | tf_op jit(solution)/shard_map/all_gather | solution.py:161
  72.4 179.6 %copy-start.41 = (f32[1536]{0:T(1024)}, f32[1536]{0:T(1024)S(1)}, u32[]{:S(2)}) copy-start(f32[1536]{0:T(1024)S(1)} %convert_element_type.213) | copy-start | bytes 18436
  156.7 16.6 %copy-start.45 = (s32[256]{0:T(256)S(1)}, s32[256]{0:T(256)}, u32[]{:S(2)}) copy-start(s32[256]{0:T(256)} %get-tuple-element.1088) | copy-start | bytes 3076
  156.7 16.6 %copy-start.48 = (s32[8]{0:T(128)S(1)}, s32[8]{0:T(128)}, u32[]{:S(2)}) copy-start(s32[8]{0:T(128)} %param.19) | copy-start | bytes 100
  190.4 10.7 copy-start.23
  226.0 10.6 copy-start.23
  253.6 15.7 copy-start.36
  269.3 177.6 %all-to-all-start.2 = ((bf16[16,160,1536]{2,1,0:T(8,128)(2,1)}), bf16[16,160,1536]{2,1,0:T(8,128)(2,1)}, u32[]{:S(2)}, u32[]{:S(2)}) async-start(bf16[16,160,1536]{2,1,0:T(8,128)(2,1)} %bitcast.308), calls=%async_computation.2 | async-start | bytes 15728640 | tf_op jit(solution)/shard_map/all_to_all | solution.py:283
  446.9 177.7 %all-to-all-start = ((bf16[16,160,1536]{2,1,0:T(8,128)(2,1)}), bf16[16,160,1536]{2,1,0:T(8,128)(2,1)}, u32[]{:S(2)}, u32[]{:S(2)}) async-start(bf16[16,160,1536]{2,1,0:T(8,128)(2,1)} %broadcast_multiply_fusion), calls=%async_computation | async-start | bytes 15728640 | tf_op jit(solution)/shard_map/all_to_all | solution.py:265
  631.8 15.5 slice-start
  706.3 178.0 %all-to-all-start.1 = ((bf16[2,1280,1536]{2,0,1:T(2,128)(2,1)}), bf16[2,1280,1536]{2,0,1:T(2,128)(2,1)}, u32[]{:S(2)}, u32[]{:S(2)}) async-start(bf16[2,1280,1536]{2,0,1:T(2,128)(2,1)} %copy.158), calls=%async_computation.1 | async-start | bytes 15728640 | tf_op jit(solution)/shard_map/all_to_all | solution.py:267
  884.3 177.6 %all-to-all-start.3 = ((bf16[2,1280,1536]{2,0,1:T(2,128)(2,1)}), bf16[2,1280,1536]{2,0,1:T(2,128)(2,1)}, u32[]{:S(2)}, u32[]{:S(2)}) async-start(bf16[2,1280,1536]{2,0,1:T(2,128)(2,1)} %copy.162), calls=%async_computation.3 | async-start | bytes 15728640 | tf_op jit(solution)/shard_map/all_to_all | solution.py:288
  889.3 364.7 %reduce-scatter.9.cloned.1.call-start = ((), (), s32[]{:S(2)}) async-start(), calls=%async_computation.14 | async-start | bytes 1310720 | tf_op jit(solution)/shard_map/reduce_scatter | solution.py:374
  897.3 17.9 %copy-start.13 = (f32[256,1536]{1,0:T(8,128)S(1)}, f32[256,1536]{1,0:T(8,128)}, u32[]{:S(2)}) copy-start(f32[256,1536]{1,0:T(8,128)} %convert_multiply_fusion.2) | copy-start | bytes 4718596
  924.8 170.2 %copy-start.39 = (f32[256,16]{0,1:T(8,128)}, f32[256,16]{0,1:T(8,128)S(1)}, u32[]{:S(2)}) copy-start(f32[256,16]{0,1:T(8,128)S(1)} %select_reduce_fusion.2) | copy-start | bytes 49156
  924.9 170.1 %copy-start.56 = (f32[256]{0:T(256)}, f32[256]{0:T(256)S(1)}, u32[]{:S(2)}) copy-start(f32[256]{0:T(256)S(1)} %multiply_reduce_fusion.4) | copy-start | bytes 3076
  1087.9 10.4 slice-start.2
  1166.5 92.4 %reduce-scatter.11.cloned.1.call-start = ((), (), s32[]{:S(2)}) async-start(), calls=%async_computation.15 | async-start | bytes 1310720 | tf_op jit(solution)/shard_map/reduce_scatter | solution.py:377
  1177.7 180.1 %reduce-scatter.15.cloned.1.call-start = ((), (), s32[]{:S(2)}) async-start(), calls=%async_computation.17 | async-start | bytes 11796480
  1236.6 369.1 %reduce-scatter.13.cloned.1.call-start = ((), (), s32[]{:S(2)}) async-start(), calls=%async_computation.16 | async-start | bytes 26763264
  1376.0 236.7 %copy-start.1 = (bf16[2,1536,512]{2,1,0:T(8,128)(2,1)S(1)}, bf16[2,1536,512]{2,1,0:T(8,128)(2,1)}, u32[]{:S(2)}) copy-start(bf16[2,1536,512]{2,1,0:T(8,128)(2,1)} %param.30) | copy-start | bytes 9437188
  (57 other events, 256.5 us)
Sparse Core Ops, SparseCore 0:
  9.7 28.0 all-gather.13
  39.4 24.4 all-gather.7
  66.3 26.1 all-gather.15
  94.0 51.7 all-gather.11
  148.0 25.2 all-gather.9
  174.9 51.7 all-gather.17
  1166.6 25.6 reduce-scatter.8
  1195.5 27.7 reduce-scatter.10
  1236.7 93.2 reduce-scatter.14
  1355.0 250.6 reduce-scatter.12
where the time goes:
time: 1630 us; the launch traced here: 1620 us
  waiting for transfers between devices  879 us (54%)
  local copies, waits for them, and re-layouts  354 us (22%)
  matrix products  219 us (13%)
  other arithmetic  97.1 us (6%)
  blocking collectives  32.7 us (2%)
  starting transfers between devices  21.2 us (1%)
  between operations  16.3 us (1%)
    unnamed x12, waiting for transfers between devices  226 us
    all_to_all x1, waiting for transfers between devices, body(): lax.all_to_all(dispatched, 'fsdp', split_axis=0, concat_axis=1, tiled=True)  166 us
    all_to_all x1, waiting for transfers between devices, body(): lax.all_to_all(local_grad_in, 'fsdp', split_axis=1, concat_axis=0, tiled=...  137 us
    all_to_all x1, waiting for transfers between devices, body(): lax.all_to_all(local_out, 'fsdp', split_axis=1, concat_axis=0, tiled=True)  133 us
    all_to_all x1, waiting for transfers between devices, body(): lax.all_to_all(grad_slots, 'fsdp', split_axis=0, concat_axis=1, tiled=True)  132 us
    unnamed x137, local copies, waits for them, and re-layouts  92.8 us
    concatenate x1, local copies, waits for them, and re-layouts, body(): jnp.concatenate([lax.dot_general(attn_in, grad_query_lin, CONTRACT_FIRST,...  61.3 us
    convert_element_type x1, local copies, waits for them, and re-layouts, expert_forward(): expert_out = jnp.einsum('ecf,edf->ecd', hidden, w_down, preferred_element...  43.7 us
  transfers between devices with their start and end apart: 14, of which 9 were waited for; matrix products, arithmetic and copies ran while one was open for 28% of the time, Pallas kernels for 0%

commit v1 on v0

v1 whole, which is shorter than its diff:
```python
import functools
import math

import jax
import jax.numpy as jnp
from jax import lax
from jax.experimental import pallas as pl
from jax.experimental.pallas import tpu as pltpu
from jax.sharding import PartitionSpec as P

HEAD = 64
HALF = HEAD // 2
NORM_EPS = 1e-06
ATTN_SCALE = 0.015625
RESID_SCALE = 0.22
ROPE_THETA = 10000.0
MASKED_SCORE = -1e30
LANES = 128
LAST = (((1,), (1,)), ((), ()))
FIRST = (((0,), (0,)), ((), ()))
F32 = jnp.float32
BF16 = jnp.bfloat16
VMEM = pl.BlockSpec(memory_space=pltpu.VMEM)
SMEM = pl.BlockSpec(memory_space=pltpu.SMEM)


def params(mib=60, **kw):
    return pltpu.CompilerParams(vmem_limit_bytes=mib * 2**20, **kw)


def call(kernel, outs, ins, scratch=(), flops=0):
    size = lambda v: v.size * v.dtype.itemsize
    return pl.pallas_call(
        kernel,
        out_shape=outs,
        in_specs=[SMEM] + [VMEM] * (len(ins) - 1),
        out_specs=[VMEM] * len(outs),
        scratch_shapes=list(scratch),
        compiler_params=params(),
        cost_estimate=pl.CostEstimate(
            flops=flops, bytes_accessed=sum(map(size, list(ins) + list(outs))), transcendentals=0
        ),
    )(*ins)


def shape(dims, dtype):
    return jax.ShapeDtypeStruct(tuple(dims), dtype)


def dot(a, b, dims=(((1,), (0,)), ((), ()))):
    return lax.dot_general(a, b, dims, preferred_element_type=F32)


def scale_of(x):
    return lax.rsqrt(jnp.mean(x * x, axis=-1, keepdims=True) + NORM_EPS)


def gain_row(misc_ref, column):
    return misc_ref[...].astype(F32).T[column : column + 1, :]


def span_rows(spans, index, size):
    return pl.ds(pl.multiple_of(spans[index] * size, size), size)


def rope(front, back, cosine, sine):
    return jnp.concatenate([front * cosine - back * sine, back * cosine + front * sine], axis=-1)


def unrope(front, back, cosine, sine):
    return jnp.concatenate([front * cosine + back * sine, back * cosine - front * sine], axis=-1)


def project_kernel(count, heads, kv_heads, experts, spans, *refs):
    pieces = refs[:count]
    weight, misc, cosine, sine, attn_in, query, key, value = refs[count:]
    gain = gain_row(misc, experts)
    size = pieces[0].shape[0] // 2
    for j in range(count):
        x = pieces[j][...].astype(F32)
        rows_in = (x * scale_of(x) * gain).astype(BF16)
        lin = dot(rows_in, weight[...])
        for h in range(2):
            at = span_rows(spans, 2 * j + h, size)
            cut = slice(h * size, (h + 1) * size)
            attn_in[at, :] = rows_in[cut]
            cos, sin = cosine[at, :], sine[at, :]
            for i in range(heads + kv_heads):
                lo = i * HEAD
                turned = rope(lin[cut, lo : lo + HALF], lin[cut, lo + HALF : lo + HEAD], cos, sin)
                if i < heads:
                    query[i, at, :] = (turned * ATTN_SCALE).astype(BF16)
                else:
                    key[i - heads, at, :] = turned.astype(BF16)
            for i in range(kv_heads):
                lo = (heads + kv_heads + i) * HEAD
                value[i, at, :] = lin[cut, lo : lo + HEAD].astype(BF16)


def diagonal(size, group):
    keys = lax.broadcasted_iota(jnp.int32, (size, group * size), 0)
    queries = lax.broadcasted_iota(jnp.int32, (size, group * size), 1) % size
    return keys <= queries


def scores_of(key_rows, query_rows, keep, size):
    raw = dot(key_rows, query_rows, LAST)
    seen = raw.shape[0] - size
    last = jnp.where(keep, raw[seen:], MASKED_SCORE)
    return last if seen == 0 else jnp.concatenate([raw[:seen], last], axis=0)


def attend_kernel(count, spans, query, key, value, w_out, mix, lse, *parts):
    kv_heads, length, _ = key.shape
    group = query.shape[0] // kv_heads
    blocks = 2 * count
    size = length // blocks
    keep = diagonal(size, group)
    for g in range(kv_heads):
        for i in range(blocks):
            rows = slice(i * size, (i + 1) * size)
            seen = (i + 1) * size
            q = query[g * group : (g + 1) * group, rows, :].reshape(group * size, HEAD)
            scores = scores_of(key[g, :seen, :], q, keep, size)
            top = jnp.max(scores, axis=0, keepdims=True)
            grown = jnp.exp(scores - top)
            total = jnp.sum(grown, axis=0, keepdims=True)
            mixed = dot(value[g, :seen, :], grown.astype(BF16), FIRST) / total
            lse[g, i, :, :] = top + jnp.log(total)
            for r in range(group):
                lo = (g * group + r) * HEAD
                mix[rows, lo : lo + HEAD] = mixed[:, r * size : (r + 1) * size].T.astype(BF16)
    for j in range(count):
        own = jnp.concatenate([mix[span_rows(spans, 2 * j + h, size), :] for h in range(2)], axis=0)
        parts[j][...] = dot(own, w_out[...], LAST).astype(parts[j].dtype)


def norm_two_kernel(experts, _, x, misc, *refs):
    parts, (after, ffn_in) = refs[:-2], refs[-2:]
    branch = sum(p[...].astype(F32) for p in parts)
    rows = x[...].astype(F32) + RESID_SCALE * branch
    after[...] = rows
    ffn_in[...] = (rows * scale_of(rows) * gain_row(misc, experts + 1)).astype(BF16)


def router_probs(rows, router, experts):
    logits = dot(rows, router)
    lane = lax.broadcasted_iota(jnp.int32, logits.shape, 1)
    logits = jnp.where(lane < experts, logits, MASKED_SCORE)
    grown = jnp.exp(logits - jnp.max(logits, axis=-1, keepdims=True))
    return grown / jnp.sum(grown, axis=-1, keepdims=True), lane


def experts_kernel(
    experts, cap, me, rows_ref, grad_ref, w_gate, w_up, w_down, misc,
    mix_ref, back_ref, disp, slots, grad_gate, grad_up, hidden_ref, keys
):
    local = w_gate.shape[0]
    width = w_gate.shape[1]
    rows = rows_ref[...]
    count = rows.shape[0] // 2
    probs, lane = router_probs(rows, misc[...], experts)
    keys[...] = grad_ref[:, width:].astype(F32).T
    grad = grad_ref[:, :width].astype(F32) * RESID_SCALE
    slot = lax.broadcasted_iota(jnp.int32, (cap, count), 0).astype(F32)
    mixed = [jnp.zeros((count, width), F32)] * 2
    back = [jnp.zeros((count, width), F32)] * 2
    notes = [jnp.zeros((count, LANES), F32)] * 2
    for e in range(local):
        name = me[0] * local + e
        key = keys[pl.ds(name, 1), :]
        share = jnp.sum(jnp.where(lane == name, probs, 0.0), axis=-1, keepdims=True)
        scaled = (grad * share).astype(BF16)
        picks = [(slot == key[:, b * count : (b + 1) * count]).astype(BF16) for b in range(2)]
        cuts = [slice(b * count, (b + 1) * count) for b in range(2)]
        mine = jnp.concatenate([dot(picks[b], rows[cuts[b]]) for b in range(2)], 0).astype(BF16)
        grads = jnp.concatenate([dot(picks[b], scaled[cuts[b]]) for b in range(2)], 0).astype(BF16)
        disp[e, 0] = mine
        slots[e, 0] = grads
        gate, up = dot(mine, w_gate[e]), dot(mine, w_up[e])
        sigmoid = 1.0 / (1.0 + jnp.exp(-gate))
        silu = gate * sigmoid
        hidden = (silu * up).astype(BF16)
        hidden_ref[e, 0] = hidden
        out = dot(hidden, w_down[e], LAST).astype(BF16)
        grad_hidden = dot(grads, w_down[e])
        d_gate = (grad_hidden * up * sigmoid * (1.0 + gate * (1.0 - sigmoid))).astype(BF16)
        d_up = (grad_hidden * silu).astype(BF16)
        grad_gate[e, 0] = d_gate
        grad_up[e, 0] = d_up
        d_in = (dot(d_gate, w_gate[e], LAST) + dot(d_up, w_up[e], LAST)).astype(BF16)
        for b in range(2):
            at = slice(b * cap, (b + 1) * cap)
            picked = dot(picks[b], out[at], FIRST)
            mixed[b] = mixed[b] + share[cuts[b]] * picked
            note = jnp.sum(grad[cuts[b]] * picked, axis=-1, keepdims=True)
            high = note.astype(BF16).astype(F32)
            notes[b] = (
                notes[b]
                + jnp.where(lane[cuts[b]] == name, high, 0.0)
                + jnp.where(lane[cuts[b]] == name + LANES // 2, note - high, 0.0)
            )
            back[b] = back[b] + dot(picks[b], d_in[at], FIRST)
    for b in range(2):
        at = slice(b * count, (b + 1) * count)
        mix_ref[at, :] = mixed[b].astype(BF16)
        back_ref[at, :width] = back[b].astype(BF16)
        back_ref[at, width:] = notes[b].astype(BF16)


def expert_terms_kernel(disp, slots, grad_gate, grad_up, hidden, out):
    count, _, _, depth, _ = out.shape
    pairs = ((disp, grad_gate), (disp, grad_up), (slots, hidden))
    for i, (left, right) in enumerate(pairs):
        full = dot(left[0], right[0], FIRST).astype(BF16)
        for c in range(count):
            out[c, i, 0] = full[c * depth : (c + 1) * depth]


def norm_two_back_kernel(experts, _, back, cotangent, after, misc, grad_after, grad_branch, terms):
    width = after.shape[1]
    rows = after[...]
    scale = scale_of(rows)
    normed = rows * scale
    gain = gain_row(misc, experts + 1)
    ffn_in = (normed * gain).astype(BF16)
    probs, lane = router_probs(ffn_in, misc[...], experts)
    notes = back[:, width:].astype(F32)
    notes = notes + pltpu.roll(notes, LANES // 2, 1)
    notes = jnp.where(lane < experts, notes, 0.0)
    logits = probs * (notes - jnp.sum(probs * notes, axis=-1, keepdims=True))
    high = logits.astype(BF16)
    low = (logits - high.astype(F32)).astype(BF16)
    grad_in = back[:, :width].astype(F32) + dot(high, misc[...], LAST) + dot(low, misc[...], LAST)
    grad_gain = jnp.sum(grad_in * normed, axis=0, keepdims=True)
    line = lax.broadcasted_iota(jnp.int32, (LANES, width), 0)
    terms[...] = (
        dot(ffn_in, high, FIRST)
        + dot(ffn_in, low, FIRST)
        + jnp.where(line == experts + 1, grad_gain, 0.0).T
    )
    scaled = grad_in * gain
    grad = cotangent[...].astype(F32) + scale * (
        scaled - normed * jnp.mean(scaled * normed, axis=-1, keepdims=True)
    )
    grad_after[...] = grad
    grad_branch[...] = (RESID_SCALE * grad).astype(BF16)


def attend_back_kernel(count, spans, *refs):
    pieces = refs[:count]
    w_out, query, key, value, lse, cosine, sine, lin, grads, key_sum, value_sum = refs[count:]
    kv_heads, length, _ = key.shape
    heads = query.shape[0]
    group = heads // kv_heads
    blocks = 2 * count
    size = length // blocks
    keep = diagonal(size, group)
    for j in range(count):
        rows = dot(pieces[j][...], w_out[...]).astype(BF16)
        for h in range(2):
            at = span_rows(spans, 2 * j + h, size)
            for i in range(heads):
                grads[i, at, :] = rows[h * size : (h + 1) * size, i * HEAD : (i + 1) * HEAD]
    for g in range(kv_heads):
        key_sum[...] = jnp.zeros_like(key_sum)
        value_sum[...] = jnp.zeros_like(value_sum)
        for i in range(blocks):
            rows = slice(i * size, (i + 1) * size)
            seen = (i + 1) * size
            q = query[g * group : (g + 1) * group, rows, :].reshape(group * size, HEAD)
            grad = grads[g * group : (g + 1) * group, rows, :].reshape(group * size, HEAD)
            probs = jnp.exp(scores_of(key[g, :seen, :], q, keep, size) - lse[g, i])
            grad_probs = dot(value[g, :seen, :], grad, LAST)
            delta = jnp.sum(probs * grad_probs, axis=0, keepdims=True)
            raw = (probs * (grad_probs - delta)).astype(BF16)
            value_sum[:seen, :] += dot(probs.astype(BF16), grad)
            key_sum[:seen, :] += dot(raw, q)
            grad_query = dot(key[g, :seen, :], raw, FIRST) * ATTN_SCALE
            for r in range(group):
                turned = grad_query[:, r * size : (r + 1) * size].T
                lo = (g * group + r) * HEAD
                lin[rows, lo : lo + HEAD] = unrope(
                    turned[:, :HALF], turned[:, HALF:], cosine[rows, :], sine[rows, :]
                ).astype(BF16)
        lo = (heads + g) * HEAD
        lin[:, lo : lo + HEAD] = unrope(
            key_sum[:, :HALF], key_sum[:, HALF:], cosine[...], sine[...]
        ).astype(BF16)
        lo = (heads + kv_heads + g) * HEAD
        lin[:, lo : lo + HEAD] = value_sum[...].astype(BF16)


def input_terms_kernel(count, spans, lin, weight, *parts):
    size = lin.shape[0] // (2 * count)
    for j in range(count):
        own = jnp.concatenate([lin[span_rows(spans, 2 * j + h, size), :] for h in range(2)], axis=0)
        parts[j][...] = dot(own, weight[...], LAST).astype(parts[j].dtype)


def weight_terms_kernel(count, experts, spans, *refs):
    pieces = refs[:count]
    attn_in, lin, mix, weight, misc, more, out, branch = refs[count:]
    length, width = attn_in.shape
    size = length // (2 * count)
    for j in range(count):
        for h in range(2):
            branch[span_rows(spans, 2 * j + h, size), :] = pieces[j][h * size : (h + 1) * size, :]
    step = width // count
    lane = lax.broadcasted_iota(jnp.int32, (step, LANES), 1)
    for c in range(count):
        cut = slice(c * step, (c + 1) * step)
        attn = dot(attn_in[:, cut], lin[...], FIRST)
        outs = dot(branch[:, cut], mix[...], FIRST)
        gain = misc[cut, :].astype(F32)[:, experts : experts + 1]
        grad_gain = jnp.sum(weight[cut, :].astype(F32) * attn, axis=-1, keepdims=True) / gain
        notes = more[cut, :] + jnp.where(lane == experts, grad_gain, 0.0)
        high = notes.astype(BF16).astype(F32)
        notes = high + pltpu.roll(jnp.where(lane < LANES // 2, notes - high, 0.0), LANES // 2, 1)
        full = jnp.concatenate([attn, outs, notes], axis=1).astype(BF16)
        if len(out.shape) == 2:
            out[cut, :] = full
        else:
            each = out.shape[2]
            for f in range(out.shape[0]):
                out[f, c] = full[f * each : (f + 1) * each]


def norm_one_back_kernel(experts, _, x, misc, grad_after, *refs):
    parts, grad_in = refs[:-1], refs[-1]
    grad = sum(p[...].astype(F32) for p in parts) * gain_row(misc, experts)
    rows = x[...].astype(F32)
    scale = scale_of(rows)
    normed = rows * scale
    grad_in[...] = grad_after[...] + scale * (
        grad - normed * jnp.mean(grad * normed, axis=-1, keepdims=True)
    )


def split_kernel(experts, widths, _, terms, query, key, value, out, notes):
    count = terms.shape[0]
    for s in range(count):
        lo = 0
        for ref, wide in zip((query, key, value, out), widths):
            ref[:, s * wide : (s + 1) * wide] = terms[s, :, lo : lo + wide].astype(F32)
            lo += wide
    total = sum(terms[s, :, lo:].astype(F32) for s in range(count))
    notes[...] = total + pltpu.roll(total, LANES // 2, 1)


def exchange(value, axis, offset):
    n = lax.axis_size(axis)
    return lax.ppermute(value, axis, [(i, i ^ offset) for i in range(n)])


def slot_keys(route_rows, experts):
    hits = (route_rows[:, :, None] == jnp.arange(experts, dtype=jnp.int32)).any(axis=1)
    rows = jnp.arange(route_rows.shape[0], dtype=jnp.int32)
    earlier = (rows[None, :] < rows[:, None]).astype(BF16)
    ranks = jnp.dot(earlier, hits.astype(BF16), preferred_element_type=F32)
    keys = jnp.where(hits, ranks, -1.0).astype(BF16)
    return jnp.pad(keys, ((0, 0), (0, LANES - experts)), constant_values=-1)


def body(
    hidden_in, span_order, routes, attn_gain, query_weight, key_weight, value_weight, out_weight,
    ffn_gain, router_weight, gate_weight, up_weight, down_weight, cotangent
):
    ctx, fsdp = lax.axis_size("ctx"), lax.axis_size("fsdp")
    me_ctx, me_fsdp = lax.axis_index("ctx"), lax.axis_index("fsdp")
    x = hidden_in[0]
    count, width = x.shape
    length = ctx * count
    heads = query_weight.shape[1] // HEAD // ctx
    kv_heads = key_weight.shape[1] // HEAD // ctx
    experts = router_weight.shape[1]
    local, _, units = gate_weight.shape
    cap = count * routes.shape[2] * 5 // (4 * experts)
    q_wide, kv_wide = heads * HEAD, kv_heads * HEAD
    lin_wide = q_wide + 2 * kv_wide
    chips = fsdp // 2
    no_scalars = jnp.zeros((1,), jnp.int32)

    own = lambda w, wide: lax.dynamic_slice_in_dim(w, me_ctx * wide, wide, 1)
    pack = jnp.concatenate(
        [
            own(query_weight, q_wide),
            own(key_weight, kv_wide),
            own(value_weight, kv_wide),
            own(out_weight, q_wide),
            router_weight,
            attn_gain[:, None],
            ffn_gain[:, None],
            jnp.zeros((attn_gain.shape[0], LANES - experts - 2), BF16),
        ],
        axis=1,
    )
    pack = lax.all_gather(pack, "fsdp", axis=0, tiled=True)
    w_lin, w_out, misc = (
        pack[:, :lin_wide],
        pack[:, lin_wide : lin_wide + q_wide],
        pack[:, lin_wide + q_wide :],
    )
    pieces = [x] + [exchange(x, "ctx", j) for j in range(1, ctx)]
    owners = jnp.stack([me_ctx ^ j for j in range(ctx)])
    spans = span_order.reshape(ctx, 2)[owners].reshape(-1)
    keys = slot_keys(routes[0], experts)
    grad_pack = lax.all_gather(
        jnp.concatenate([cotangent[0], keys], axis=1), "fsdp", axis=0, tiled=True
    )
    frequencies = ROPE_THETA ** (-2.0 * jnp.arange(HALF, dtype=F32) / HEAD)
    angles = jnp.arange(length, dtype=F32)[:, None] * frequencies[None, :]
    cosine, sine = jnp.cos(angles), jnp.sin(angles)

    attn_in, query, key, value = call(
        functools.partial(project_kernel, ctx, heads, kv_heads, experts),
        [
            shape((length, width), BF16),
            shape((heads, length, HEAD), BF16),
            shape((kv_heads, length, HEAD), BF16),
            shape((kv_heads, length, HEAD), BF16),
        ],
        [spans, *pieces, w_lin, misc, cosine, sine],
        flops=2 * length * width * lin_wide,
    )
    part_types = [shape((count, width), F32 if j == 0 else BF16) for j in range(ctx)]
    mix, lse, *parts = call(
        functools.partial(attend_kernel, ctx),
        [
            shape((length, q_wide), BF16),
            shape((kv_heads, 2 * ctx, 1, heads // kv_heads * length // (2 * ctx)), F32),
            *part_types,
        ],
        [spans, query, key, value, w_out],
        flops=8 * length * length * q_wide,
    )
    parts = [parts[0]] + [exchange(parts[j], "ctx", j) for j in range(1, ctx)]
    after, ffn_in = call(
        functools.partial(norm_two_kernel, experts),
        [shape((count, width), F32), shape((count, width), BF16)],
        [no_scalars, x, misc, *parts],
    )
    rows_all = lax.all_gather(ffn_in, "fsdp", axis=0, tiled=True)

    whole = lambda *dims: pl.BlockSpec(
        dims, lambda i, me: (0,) * len(dims), pipeline_mode=pl.Buffered(1)
    )
    lines = lambda wide: pl.BlockSpec((2 * count, wide), lambda i, me: (i, 0))
    stored = lambda wide: pl.BlockSpec((local, 1, 2 * cap, wide), lambda i, me: (0, i, 0, 0))
    mix_part, back_part, *saved = pl.pallas_call(
        functools.partial(experts_kernel, experts, cap),
        out_shape=[
            shape((fsdp * count, width), BF16),
            shape((fsdp * count, width + LANES), BF16),
            *[shape((local, chips, 2 * cap, w), BF16) for w in (width, width, units, units, units)],
        ],
        grid_spec=pltpu.PrefetchScalarGridSpec(
            num_scalar_prefetch=1,
            grid=(chips,),
            in_specs=[
                lines(width),
                lines(width + LANES),
                *[whole(local, width, units)] * 3,
                whole(width, LANES),
            ],
            out_specs=[
                lines(width),
                lines(width + LANES),
                *[stored(w) for w in (width, width, units, units, units)],
            ],
            scratch_shapes=[pltpu.VMEM((LANES, 2 * count), F32)],
        ),
        compiler_params=params(),
        cost_estimate=pl.CostEstimate(
            flops=16 * local * fsdp * cap * width * units,
            bytes_accessed=60 * 2**20,
            transcendentals=0,
        ),
    )(me_fsdp[None], rows_all, grad_pack, gate_weight, up_weight, down_weight, misc)

    back = lax.psum_scatter(back_part, "fsdp", scatter_dimension=0, tiled=True)
    mixture = lax.psum_scatter(mix_part, "fsdp", scatter_dimension=0, tiled=True)
    hidden_out = (after + RESID_SCALE * mixture.astype(F32)).astype(BF16)[None]

    depth = width // ctx
    slots = fsdp * cap
    saved = [s.reshape(local, slots, s.shape[-1]) for s in saved]
    step = math.lcm(depth, LANES)
    tall = pl.BlockSpec((1, slots, step), lambda e, c: (e, 0, c))
    thin = pl.BlockSpec((1, slots, units), lambda e, c: (e, 0, 0))
    expert_terms = pl.pallas_call(
        expert_terms_kernel,
        out_shape=shape((ctx, 3, local, depth, units), BF16),
        grid=(local, width // step),
        in_specs=[tall, tall, thin, thin, thin],
        out_specs=pl.BlockSpec((step // depth, 3, 1, depth, units), lambda e, c: (c, 0, e, 0, 0)),
        compiler_params=params(),
        cost_estimate=pl.CostEstimate(
            flops=6 * local * slots * width * units, bytes_accessed=40 * 2**20, transcendentals=0
        ),
    )(*saved)
    expert_sums = lax.psum_scatter(
        expert_terms.reshape(-1, units), "ctx", scatter_dimension=0, tiled=True
    ).reshape(3, local, depth, units)
    grad_gate, grad_up, grad_down = (expert_sums[i].astype(F32) for i in range(3))

    grad_after, grad_branch, more = call(
        functools.partial(norm_two_back_kernel, experts),
        [shape((count, width), F32), shape((count, width), BF16), shape((width, LANES), F32)],
        [no_scalars, back, cotangent[0], after, misc],
    )
    branches = [grad_branch] + [exchange(grad_branch, "ctx", j) for j in range(1, ctx)]
    [lin] = call(
        functools.partial(attend_back_kernel, ctx),
        [shape((length, lin_wide), BF16)],
        [spans, *branches, w_out, query, key, value, lse, cosine, sine],
        scratch=[
            pltpu.VMEM((heads, length, HEAD), BF16),
            pltpu.VMEM((length, HEAD), F32),
            pltpu.VMEM((length, HEAD), F32),
        ],
        flops=20 * length * length * q_wide,
    )
    in_parts = call(
        functools.partial(input_terms_kernel, ctx),
        part_types,
        [spans, lin, w_lin],
        flops=2 * length * width * lin_wide,
    )
    in_parts = [in_parts[0]] + [exchange(in_parts[j], "ctx", j) for j in range(1, ctx)]
    total_wide = lin_wide + q_wide + LANES
    each = width // (ctx * fsdp)
    direct = each % 16 == 0
    [terms] = call(
        functools.partial(weight_terms_kernel, ctx, experts),
        [shape((fsdp, ctx, each, total_wide) if direct else (width, total_wide), BF16)],
        [spans, *branches, attn_in, lin, mix, w_lin, misc, more],
        scratch=[pltpu.VMEM((length, width), BF16)],
        flops=2 * length * width * (lin_wide + q_wide),
    )
    if not direct:
        terms = terms.reshape(ctx, fsdp, each, total_wide).swapaxes(0, 1)
    terms = lax.psum_scatter(terms, "fsdp", scatter_dimension=0, tiled=True)[0]
    terms = lax.all_to_all(terms, "ctx", split_axis=0, concat_axis=0, tiled=True)
    grad_query, grad_key, grad_value, grad_out, notes = call(
        functools.partial(split_kernel, experts, (q_wide, kv_wide, kv_wide, q_wide)),
        [
            *[shape((each, ctx * w), F32) for w in (q_wide, kv_wide, kv_wide, q_wide)],
            shape((each, LANES), F32),
        ],
        [no_scalars, terms],
    )
    [grad_in] = call(
        functools.partial(norm_one_back_kernel, experts),
        [shape((count, width), F32)],
        [no_scalars, x, misc, grad_after, *in_parts],
    )
    return (
        hidden_out,
        grad_in[None],
        notes[:, experts],
        grad_query,
        grad_key,
        grad_value,
        grad_out,
        notes[:, experts + 1],
        notes[:, :experts],
        grad_gate,
        grad_up,
        grad_down,
    )


def solution(mesh):
    rows, both = P("fsdp", "ctx", None), ("ctx", "fsdp")
    split = P("fsdp", None)
    return jax.shard_map(
        body,
        mesh=mesh,
        in_specs=(
            rows, P(), rows, P("fsdp"), split, split, split, split, P("fsdp"), split,
            P("fsdp", None, None), P("fsdp", None, None), P("fsdp", None, None), rows,
        ),
        out_specs=(
            rows, rows, P(both), P(both, None), P(both, None), P(both, None), P(both, None),
            P(both), P(both, None), rows, rows, rows,
        ),
        check_vma=False,
    )
```

time: 1630 us -> 635 us (0.39)
  waiting for transfers between devices: 879 us -> 406 us
  local copies, waits for them, and re-layouts: 354 us -> 23.3 us
  matrix products: 219 us -> 0.16 us
  Pallas kernels: 0 us -> 150 us
  other arithmetic: 97.1 us -> 10.2 us
  blocking collectives: 32.7 us -> 0 us
    all_to_all x4 -> x1, waiting for transfers between devices: 567 us -> 0.01 us  [body(): lax.all_to_all(terms, 'ctx', split_axis=0, concat_axis=0, tiled=True)]
    reduce_scatter x2 -> x4, waiting for transfers between devices: 0.01 us -> 243 us  [the longest x1 88.7 us: body(): lax.psum_scatter(expert_terms.reshape(-1, units), 'ctx', scatter_dimensio...]
    unnamed x12 -> x7, waiting for transfers between devices: 226 us -> 0.62 us
    dot_general x40 -> x1, matrix products: 219 us -> 0.16 us  [slot_keys(): ranks = jnp.dot(earlier, hits.astype(BF16), preferred_element_type=F32)]
    pallas_call x0 -> x11, Pallas kernels: none -> 150 us  [the longest x9 79.6 us: call(): pl.pallas_call(kernel, out_shape=outs, in_specs=[SMEM] + [VMEM] * (len(in...]
    unnamed x137 -> x32, local copies, waits for them, and re-layouts: 92.8 us -> 7.22 us
    ppermute x0 -> x12, waiting for transfers between devices: none -> 66.3 us  [exchange(): return lax.ppermute(value, axis, [(i, i ^ offset) for i in range(n)])]
    concatenate x1, local copies, waits for them, and re-layouts: 61.3 us -> 0.91 us  [body(): jnp.concatenate([own(query_weight, q_wide), own(key_weight, kv_wide), own...]
  transfers between devices with their start and end apart: 14 -> 20, of which waited for: 9 -> 11; matrix products, arithmetic and copies ran while one was open for 28% -> 3% of each run, Pallas kernels for 0% -> 10%
where the time goes in v1:
time: 635 us; the launch traced here: 624 us
  waiting for transfers between devices  406 us (64%)
  Pallas kernels  150 us (24%)
  local copies, waits for them, and re-layouts  23.3 us (4%)
  starting transfers between devices  19.4 us (3%)
  between operations  14.8 us (2%)
  other arithmetic  10.2 us (2%)
    reduce_scatter x1, waiting for transfers between devices, body(): lax.psum_scatter(expert_terms.reshape(-1, units), 'ctx', scatter_dimensio...  88.7 us
    pallas_call x9, Pallas kernels, call(): pl.pallas_call(kernel, out_shape=outs, in_specs=[SMEM] + [VMEM] * (len(in...  79.6 us
    reduce_scatter x1, waiting for transfers between devices, body(): back = lax.psum_scatter(back_part, 'fsdp', scatter_dimension=0, tiled=True)  73.4 us
    reduce_scatter x1, waiting for transfers between devices, body(): lax.psum_scatter(mix_part, 'fsdp', scatter_dimension=0, tiled=True)  67 us
    ppermute x12, waiting for transfers between devices, exchange(): return lax.ppermute(value, axis, [(i, i ^ offset) for i in range(n)])  66.3 us
    all_gather x1, waiting for transfers between devices, body(): rows_all = lax.all_gather(ffn_in, 'fsdp', axis=0, tiled=True)  62.5 us
    pallas_call x1, Pallas kernels, body(): pl.pallas_call(functools.partial(experts_kernel, experts, cap), out_shape...  50.4 us
    all_gather x1, waiting for transfers between devices, body(): pack = lax.all_gather(pack, 'fsdp', axis=0, tiled=True)  34.2 us
  transfers between devices with their start and end apart: 20, of which 11 were waited for; matrix products, arithmetic and copies ran while one was open for 3% of the time, Pallas kernels for 10%

profile of v1, /device:TPU:0, one launch (start us, length us, event | category | flops | bytes accessed | tf_op | source)
XLA Modules:
  0.0 624.4 jit_solution(1597933923438170981)
XLA Ops:
  13.9 4.0 collective-permute-start.2
  19.8 2.8 fusion.4
  22.6 34.2 %all-gather.4.cloned.1.call-done = bf16[1536,1152]{1,0:T(8,128)(2,1)} async-done(((bf16[192,1152]{1,0:T(8,128)(2,1)}), bf16[1536,1152]{1,0:T(8,128)(2,1)}) %all-gather.4.cloned.1.call-update) | async-done | bytes 3538960 | tf_op jit(solution)/shard_map/all_gather | solution.py:398
  56.8 1.8 slice.41.refs_5_.misc.refs_8_
  58.6 2.4 slice.43.w_out.refs_4_
  61.0 3.0 slice.42.refs_4_.weight.refs_7_
  65.1 13.9 %shard_map.229 = (bf16[1024,1536]{1,0:T(8,128)(2,1)}, bf16[6,1024,64]{2,1,0:T(8,128)(2,1)}, bf16[2,1024,64]{2,1,0:T(8,128)(2,1)}, bf16[2,1024,64]{2,1,0:T(8,128)(2,1)}) custom-call(s32[8]{0:T(128)} %reshape.229.spans, bf16[256,1536]{1,0:T(8,128)(2,1)} %bitcast.32, bf16[256,1536]{1,0:T(8,128)(2,1)} %collective-permute-done.refs_1_, ...), custom_call_target="tpu_custom_call" | custom-call | flops 2013265920 | bytes 10223648 | tf_op jit(solution)/shard_map/pallas_call | solution.py:33
  79.1 13.1 %shard_map.230 = (bf16[1024,384]{1,0:T(8,128)(2,1)}, f32[2,8,1,384]{3,2,1,0:T(1,128)}, f32[256,1536]{1,0:T(8,128)}, bf16[256,1536]{1,0:T(8,128)(2,1)}, bf16[256,...) custom-call(s32[8]{0:T(128)} %reshape.229.spans, bf16[6,1024,64]{2,1,0:T(8,128)(2,1)} %get-tuple-element.43.query.refs_5_, ...), custom_call_target="tpu_custom_call" | custom-call | flops 3221225472 | bytes 7233568 | tf_op jit(solution)/shard_map/pallas_call | solution.py:33
  92.2 1.6 collective-permute-start.3
  95.7 17.1 %collective-permute-done.3.refs_1_ = bf16[256,1536]{1,0:T(8,128)(2,1)S(1)} collective-permute-done((bf16[256,1536]{1,0:T(8,128)(2,1)}, bf16[256,1536]{1,0:T(8,128)(2,1)S(1)}, u32[]{:S(2)}, u32[]{:S(2)}) %collective-permute-start.3) | collective-permute-done | bytes 786464 | tf_op jit(solution)/shard_map/ppermute | solution.py:353
  112.8 17.5 %collective-permute-done.4.refs_2_ = bf16[256,1536]{1,0:T(8,128)(2,1)S(1)} collective-permute-done((bf16[256,1536]{1,0:T(8,128)(2,1)}, bf16[256,1536]{1,0:T(8,128)(2,1)S(1)}, u32[]{:S(2)}, u32[]{:S(2)}) %collective-permute-start.4) | collective-permute-done | bytes 786464 | tf_op jit(solution)/shard_map/ppermute | solution.py:353
  131.5 4.4 shard_map.231
  136.0 62.5 %all-gather.6.cloned.1.call-done.rows_ref = bf16[2048,1536]{1,0:T(8,128)(2,1)} async-done(((bf16[256,1536]{1,0:T(8,128)(2,1)}), bf16[2048,1536]{1,0:T(8,128)(2,1)}) %all-gather.6.cloned.1.call-update) | async-done | bytes 6291472 | tf_op jit(solution)/shard_map/all_gather | solution.py:443
  198.5 50.4 %shard_map.232 = (bf16[2048,1536]{1,0:T(8,128)(2,1)}, bf16[2048,1664]{1,0:T(8,128)(2,1)}, bf16[2,4,320,1536]{3,2,1,0:T(8,128)(2,1)}, bf16[2,4,320,1536]{3,2,1,0:...) custom-call(s32[1]{0:T(128)} %bitcast.6.me, ...), custom_call_target="tpu_custom_call" | custom-call | flops 32212254720 | bytes 62914560 | tf_op jit(solution)/shard_map/pallas_call | solution.py:450
  249.2 73.4 %reduce-scatter.7.cloned.1.call-done.back = bf16[256,1664]{1,0:T(8,128)(2,1)} async-done(((bf16[2048,1664]{1,0:T(8,128)(2,1)}), bf16[256,1664]{1,0:T(8,128)(2,1)}) %reduce-scatter.7.cloned.1.call-update) | async-done | bytes 851984 | tf_op jit(solution)/shard_map/reduce_scatter | solution.py:481
  322.5 5.7 shard_map.233
  328.2 2.4 collective-permute-start.8
  331.7 18.1 %collective-permute-done.8.refs_3_ = bf16[256,1536]{1,0:T(8,128)(2,1)S(1)} collective-permute-done((bf16[256,1536]{1,0:T(8,128)(2,1)}, bf16[256,1536]{1,0:T(8,128)(2,1)S(1)}, u32[]{:S(2)}, u32[]{:S(2)}) %collective-permute-start.8) | collective-permute-done | bytes 786464 | tf_op jit(solution)/shard_map/ppermute | solution.py:353
  349.8 13.5 %collective-permute-done.7.refs_2_ = bf16[256,1536]{1,0:T(8,128)(2,1)S(1)} collective-permute-done((bf16[256,1536]{1,0:T(8,128)(2,1)}, bf16[256,1536]{1,0:T(8,128)(2,1)S(1)}, u32[]{:S(2)}, u32[]{:S(2)}) %collective-permute-start.7) | collective-permute-done | bytes 786464 | tf_op jit(solution)/shard_map/ppermute | solution.py:353
  364.5 19.3 %shard_map.234.lin.refs_5_ = bf16[1024,640]{1,0:T(8,128)(2,1)} custom-call(s32[8]{0:T(128)} %reshape.229.spans, bf16[256,1536]{1,0:T(8,128)(2,1)} %get-tuple-element.55.refs_0_, bf16[256,1536]{1,0:T(8,128)(2,1)} %copy-done.6, bf16[256,1536]{1,0:T(8,128)(2,1)} %copy-done.5, bf16[256,1536]{1,0:T(8,128)(2,1)} %copy-done.4, ...), custom_call_target="tpu_custom_call" | custom-call | flops 8053063680 | bytes 7233568 | tf_op jit(solution)/shard_map/pallas_call | solution.py:33
  383.7 10.7 %shard_map.237 = bf16[8,4,48,1152]{3,2,1,0:T(8,128)(2,1)} custom-call(s32[8]{0:T(128)} %reshape.229.spans, bf16[256,1536]{1,0:T(8,128)(2,1)} %get-tuple-element.55.refs_0_, bf16[256,1536]{1,0:T(8,128)(2,1)} %copy-done.6, bf16[256,1536]{1,0:T(8,128)(2,1)} %copy-done.5, bf16[256,1536]{1,0:T(8,128)(2,1)} %copy-done.4, ...), custom_call_target="tpu_custom_call" | custom-call | flops 3221225472 | bytes 15073312 | tf_op jit(solution)/shard_map/pallas_call | solution.py:33
  395.3 20.0 %shard_map.239 = bf16[4,3,2,384,512]{4,3,2,1,0:T(8,128)(2,1)} custom-call(bf16[2,1280,1536]{2,1,0:T(8,128)(2,1)} %bitcast.44, bf16[2,1280,1536]{2,1,0:T(8,128)(2,1)} %bitcast.45, bf16[2,1280,512]{2,1,0:T(8,128)(2,1)} %bitcast.46, bf16[2,1280,512]{2,1,0:T(8,128)(2,1)} %bitcast.47, bf16[2,1280,512]{2,1,0:T(8,128)(2,1)} %bitcast.48), custom_call_target="tpu_custom_call" | custom-call | flops 12079595520 | bytes 41943040 | tf_op jit(solution)/shard_map/pallas_call | solution.py:491
  415.4 5.6 shard_map.235
  421.0 1.5 collective-permute-start.9
  424.5 13.8 %reduce-scatter.9.cloned.1.call-done = bf16[1,4,48,1152]{3,2,1,0:T(8,128)(2,1)} async-done(((bf16[8,4,48,1152]{3,2,1,0:T(8,128)(2,1)}), bf16[1,4,48,1152]{3,2,1,0:T(8,128)(2,1)}) %reduce-scatter.9.cloned.1.call-update) | async-done | bytes 442384 | tf_op jit(solution)/shard_map/reduce_scatter | solution.py:543
  438.3 3.7 all-to-all-start
  441.9 67.0 %reduce-scatter.5.cloned.1.call-done = bf16[256,1536]{1,0:T(8,128)(2,1)} async-done(((bf16[2048,1536]{1,0:T(8,128)(2,1)}), bf16[256,1536]{1,0:T(8,128)(2,1)}) %reduce-scatter.5.cloned.1.call-update) | async-done | bytes 786448 | tf_op jit(solution)/shard_map/reduce_scatter | solution.py:482
  508.9 2.2 fusion.3
  512.0 5.0 shard_map.236
  517.0 88.7 %reduce-scatter.11.cloned.1.call-done = bf16[2304,512]{1,0:T(8,128)(2,1)} async-done(((bf16[9216,512]{1,0:T(8,128)(2,1)}), bf16[2304,512]{1,0:T(8,128)(2,1)}) %reduce-scatter.11.cloned.1.call-update) | async-done | bytes 2359312 | tf_op jit(solution)/shard_map/reduce_scatter | solution.py:502
  605.7 1.8 fusion.8
  612.3 1.9 shard_map.238
  (84 shorter events, 26.8 us)
Async XLA Ops:
  7.2 5.3 copy-start.11
  7.2 5.6 copy-start.2
  7.2 49.6 %all-gather.4.cloned.1.call-start = ((), (), s32[]{:S(2)}) async-start(), calls=%async_computation.5 | async-start | bytes 3981312 | tf_op jit(solution)/shard_map/all_gather | solution.py:398
  12.4 1.4 copy-start.1
  12.4 6.1 copy-start.12
  12.4 123.5 %all-gather.8.cloned.1.call-start = ((), (), s32[]{:S(2)}) async-start(), calls=%async_computation.7 | async-start | bytes 7667712 | tf_op jit(solution)/shard_map/all_gather | solution.py:408
  13.8 184.7 %all-gather.6.cloned.1.call-start = ((), (), s32[]{:S(2)}) async-start(), calls=%async_computation.6 | async-start | bytes 7077888 | tf_op jit(solution)/shard_map/all_gather | solution.py:443
  13.9 50.1 %collective-permute-start.2 = (bf16[256,1536]{1,0:T(8,128)(2,1)S(1)}, bf16[256,1536]{1,0:T(8,128)(2,1)S(1)}, u32[]{:S(2)}, u32[]{:S(2)}) collective-permute-start(bf16[256,1536]{1,0:T(8,128)(2,1)S(1)} %bitcast.35), channel_id=1, source_target_pairs={{0,24},{8,16},{16,8},{24,0},{1,25},{9,17},{17,9},{25,1},{2,26},{10... | collective-permute-start | bytes 2359304 | tf_op jit(solution)/shard_map/ppermute | solution.py:353
  17.8 46.2 %collective-permute-start.1 = (bf16[256,1536]{1,0:T(8,128)(2,1)S(1)}, bf16[256,1536]{1,0:T(8,128)(2,1)S(1)}, u32[]{:S(2)}, u32[]{:S(2)}) collective-permute-start(bf16[256,1536]{1,0:T(8,128)(2,1)S(1)} %bitcast.36), channel_id=1, source_target_pairs={{0,16},{8,24},{16,0},{24,8},{1,17},{9,25},{17,1},{25,9},{2,18},{10... | collective-permute-start | bytes 2359304 | tf_op jit(solution)/shard_map/ppermute | solution.py:353
  18.3 45.7 %collective-permute-start = (bf16[256,1536]{1,0:T(8,128)(2,1)S(1)}, bf16[256,1536]{1,0:T(8,128)(2,1)}, u32[]{:S(2)}, u32[]{:S(2)}) collective-permute-start(bf16[256,1536]{1,0:T(8,128)(2,1)S(1)} %bitcast.37), channel_id=1, source_target_pairs={{0,8},{8,0},{16,24},{24,16},{1,9},{9,1},{17,25},{25,17},{2,10},{10... | collective-permute-start | bytes 2359304 | tf_op jit(solution)/shard_map/ppermute | solution.py:353
  64.0 1.1 copy-start.14
  92.2 20.6 %collective-permute-start.3 = (bf16[256,1536]{1,0:T(8,128)(2,1)}, bf16[256,1536]{1,0:T(8,128)(2,1)S(1)}, u32[]{:S(2)}, u32[]{:S(2)}) collective-permute-start(bf16[256,1536]{1,0:T(8,128)(2,1)} %get-tuple-element.47), channel_id=1, source_target_pairs={{0,8},{8,0},{16,24},{24,16},{1,9},{9,1},{17,25},{25,17},{2,10},{10... | collective-permute-start | bytes 2359304 | tf_op jit(solution)/shard_map/ppermute | solution.py:353
  93.8 36.5 %collective-permute-start.4 = (bf16[256,1536]{1,0:T(8,128)(2,1)}, bf16[256,1536]{1,0:T(8,128)(2,1)S(1)}, u32[]{:S(2)}, u32[]{:S(2)}) collective-permute-start(bf16[256,1536]{1,0:T(8,128)(2,1)} %get-tuple-element.48), channel_id=1, source_target_pairs={{0,16},{8,24},{16,0},{24,8},{1,17},{9,25},{17,1},{25,9},{2,18},{10... | collective-permute-start | bytes 2359304 | tf_op jit(solution)/shard_map/ppermute | solution.py:353
  95.3 35.0 %collective-permute-start.5 = (bf16[256,1536]{1,0:T(8,128)(2,1)}, bf16[256,1536]{1,0:T(8,128)(2,1)S(1)}, u32[]{:S(2)}, u32[]{:S(2)}) collective-permute-start(bf16[256,1536]{1,0:T(8,128)(2,1)} %get-tuple-element.49), channel_id=1, source_target_pairs={{0,24},{8,16},{16,8},{24,0},{1,25},{9,17},{17,9},{25,1},{2,26},{10... | collective-permute-start | bytes 2359304 | tf_op jit(solution)/shard_map/ppermute | solution.py:353
  112.8 17.5 %copy-start.8 = (bf16[256,1536]{1,0:T(8,128)(2,1)}, bf16[256,1536]{1,0:T(8,128)(2,1)S(1)}, u32[]{:S(2)}) copy-start(bf16[256,1536]{1,0:T(8,128)(2,1)S(1)} %collective-permute-done.3.refs_1_) | copy-start | bytes 2359300
  130.3 0.9 copy-start.9
  130.3 1.2 copy-start.10
  135.9 186.7 %reduce-scatter.7.cloned.1.call-start = ((), (), s32[]{:S(2)}) async-start(), calls=%async_computation.9 | async-start | bytes 7667712 | tf_op jit(solution)/shard_map/reduce_scatter | solution.py:481
  248.9 189.3 %reduce-scatter.9.cloned.1.call-start = ((), (), s32[]{:S(2)}) async-start(), calls=%async_computation.10 | async-start | bytes 3981312 | tf_op jit(solution)/shard_map/reduce_scatter | solution.py:543
  328.2 21.6 %collective-permute-start.8 = (bf16[256,1536]{1,0:T(8,128)(2,1)}, bf16[256,1536]{1,0:T(8,128)(2,1)S(1)}, u32[]{:S(2)}, u32[]{:S(2)}) collective-permute-start(bf16[256,1536]{1,0:T(8,128)(2,1)} %get-tuple-element.55.refs_0_), channel_id=1, source_target_pairs={{0,24},{8,16},{16,8},{24,0},{1,25},{9,17},{17,9},{25,1},{2,26},{10... | collective-permute-start | bytes 2359304 | tf_op jit(solution)/shard_map/ppermute | solution.py:353
  330.6 32.7 %collective-permute-start.7 = (bf16[256,1536]{1,0:T(8,128)(2,1)}, bf16[256,1536]{1,0:T(8,128)(2,1)S(1)}, u32[]{:S(2)}, u32[]{:S(2)}) collective-permute-start(bf16[256,1536]{1,0:T(8,128)(2,1)} %get-tuple-element.55.refs_0_), channel_id=1, source_target_pairs={{0,16},{8,24},{16,0},{24,8},{1,17},{9,25},{17,1},{25,9},{2,18},{10... | collective-permute-start | bytes 2359304 | tf_op jit(solution)/shard_map/ppermute | solution.py:353
  331.1 32.2 %collective-permute-start.6 = (bf16[256,1536]{1,0:T(8,128)(2,1)}, bf16[256,1536]{1,0:T(8,128)(2,1)S(1)}, u32[]{:S(2)}, u32[]{:S(2)}) collective-permute-start(bf16[256,1536]{1,0:T(8,128)(2,1)} %get-tuple-element.55.refs_0_), channel_id=1, source_target_pairs={{0,8},{8,0},{16,24},{24,16},{1,9},{9,1},{17,25},{25,17},{2,10},{10... | collective-permute-start | bytes 2359304 | tf_op jit(solution)/shard_map/ppermute | solution.py:353
  349.8 13.6 %copy-start.4 = (bf16[256,1536]{1,0:T(8,128)(2,1)}, bf16[256,1536]{1,0:T(8,128)(2,1)S(1)}, u32[]{:S(2)}) copy-start(bf16[256,1536]{1,0:T(8,128)(2,1)S(1)} %collective-permute-done.8.refs_3_) | copy-start | bytes 2359300
  363.3 0.9 copy-start.5
  363.4 1.1 copy-start.6
  394.4 114.4 %reduce-scatter.5.cloned.1.call-start = ((), (), s32[]{:S(2)}) async-start(), calls=%async_computation.8 | async-start | bytes 7077888 | tf_op jit(solution)/shard_map/reduce_scatter | solution.py:482
  395.0 210.7 %reduce-scatter.11.cloned.1.call-start = ((), (), s32[]{:S(2)}) async-start(), calls=%async_computation.11 | async-start | bytes 11796480 | tf_op jit(solution)/shard_map/reduce_scatter | solution.py:502
  415.4 93.5 %copy-start = (f32[256,1536]{1,0:T(8,128)S(1)}, f32[256,1536]{1,0:T(8,128)}, u32[]{:S(2)}) copy-start(f32[256,1536]{1,0:T(8,128)} %get-tuple-element.50.after) | copy-start | bytes 4718596
  421.0 90.1 %collective-permute-start.9 = (bf16[256,1536]{1,0:T(8,128)(2,1)}, bf16[256,1536]{1,0:T(8,128)(2,1)S(1)}, u32[]{:S(2)}, u32[]{:S(2)}) collective-permute-start(bf16[256,1536]{1,0:T(8,128)(2,1)} %get-tuple-element.58), channel_id=1, source_target_pairs={{0,8},{8,0},{16,24},{24,16},{1,9},{9,1},{17,25},{25,17},{2,10},{10... | collective-permute-start | bytes 2359304 | tf_op jit(solution)/shard_map/ppermute | solution.py:353
  422.5 88.6 %collective-permute-start.10 = (bf16[256,1536]{1,0:T(8,128)(2,1)}, bf16[256,1536]{1,0:T(8,128)(2,1)}, u32[]{:S(2)}, u32[]{:S(2)}) collective-permute-start(bf16[256,1536]{1,0:T(8,128)(2,1)} %get-tuple-element.59), channel_id=1, source_target_pairs={{0,16},{8,24},{16,0},{24,8},{1,17},{9,25},{17,1},{25,9},{2,18},{10... | collective-permute-start | bytes 2359304 | tf_op jit(solution)/shard_map/ppermute | solution.py:353
  423.5 87.6 %collective-permute-start.11 = (bf16[256,1536]{1,0:T(8,128)(2,1)}, bf16[256,1536]{1,0:T(8,128)(2,1)}, u32[]{:S(2)}, u32[]{:S(2)}) collective-permute-start(bf16[256,1536]{1,0:T(8,128)(2,1)} %get-tuple-element.60), channel_id=1, source_target_pairs={{0,24},{8,16},{16,8},{24,0},{1,25},{9,17},{17,9},{25,1},{2,26},{10... | collective-permute-start | bytes 2359304 | tf_op jit(solution)/shard_map/ppermute | solution.py:353
  438.3 173.3 %all-to-all-start = ((bf16[4,48,1152]{2,1,0:T(8,128)(2,1)}), bf16[4,48,1152]{2,1,0:T(8,128)(2,1)S(1)}, u32[]{:S(2)}, u32[]{:S(2)}) async-start(bf16[4,48,1152]{2,1,0:T(8,128)(2,1)} %bitcast.41), calls=%async_computation.3 | async-start | bytes 884736 | tf_op jit(solution)/shard_map/all_to_all | solution.py:544
  (3 other events, 2.5 us)
Sparse Core Ops, SparseCore 0:
  12.6 44.2 all-gather.3
  59.0 67.9 all-gather.7
  136.0 62.4 all-gather.5
  249.1 73.4 reduce-scatter.6
  394.5 43.6 reduce-scatter.8
  440.5 68.3 reduce-scatter.4
  512.3 93.3 reduce-scatter.10
